TPU v7x, 32 devices: a whole 2x2x4 slice. The times are simulated.
32 devices in a mesh: blk: 4 (over y, x), seq: 8 (over z, core).
Axes of the slice: x: 2, y: 2, z: 4, core: 2. Of those that a mesh axis runs over, the one named last changes fastest.
Arguments:
- tokens: bfloat16 [16, 2048, 768], P('seq', 'blk'), may hold values from -6 to 6
- seq_len: int32 [16], P('seq'), may hold values from 1024 to 2048, as said below
- ln1_gain: bfloat16 [768], P(('blk', 'seq')), may hold values from 0.5 to 1.5
- ln1_shift: bfloat16 [768], P(('blk', 'seq')), may hold values from -2.5 to 2.5
- w_qkv: bfloat16 [768, 2304], P(('blk', 'seq')), may hold values from -0.21875 to 0.21875
- w_out: bfloat16 [768, 768], P(('blk', 'seq')), may hold values from -2.5 to 2.5
- ln2_gain: bfloat16 [768], P(('blk', 'seq')), may hold values from 0.5 to 1.5
- ln2_shift: bfloat16 [768], P(('blk', 'seq')), may hold values from -2.5 to 2.5
- w_up: bfloat16 [768, 3072], P(('blk', 'seq')), may hold values from -0.21875 to 0.21875
- w_down: bfloat16 [3072, 768], P(('blk', 'seq')), may hold values from -0.109375 to 0.109375
- cotangent: bfloat16 [16, 2048, 768], P('seq', 'blk'), may hold values from -6 to 6
Outputs:
- output: bfloat16 [16, 2048, 768], P('seq', 'blk')
- grad_tokens: float32 [16, 2048, 768], P('seq', 'blk')
- grad_ln1_gain: float32 [768], P(('blk', 'seq'))
- grad_ln1_shift: float32 [768], P(('blk', 'seq'))
- grad_w_qkv: float32 [768, 2304], P(('blk', 'seq'))
- grad_w_out: float32 [768, 768], P(('blk', 'seq'))
- grad_ln2_gain: float32 [768], P(('blk', 'seq'))
- grad_ln2_shift: float32 [768], P(('blk', 'seq'))
- grad_w_up: float32 [768, 3072], P(('blk', 'seq'))
- grad_w_down: float32 [3072, 768], P(('blk', 'seq'))
Inputs may be any that keep to these rules, and one draw needn't show every extreme that they name: `seq_len`: positions at or beyond a sequence's length are padding; in every draw some sequence has exactly 2048 positions and some exactly 1024.
All inputs are finite; a program needn't handle non-finite values.
Results may differ from a plain program's by a relative error of at most 0.02.
Values may be sent and summed in bfloat16 or wider, within the bound.
A program may use at most 448 MiB of HBM per device.

v0:
```python
import jax
import jax.numpy as jnp
from jax import lax
from jax.sharding import PartitionSpec as P

HEADS = 12


def normalize(values, gain, shift):
    center = jnp.mean(values, axis=-1, keepdims=True)
    offsets = values - center
    spread = jnp.mean(offsets * offsets, axis=-1, keepdims=True)
    return offsets * lax.rsqrt(spread + 1e-05) * gain + shift


def smooth_parts(scores):
    inverse = lax.rsqrt(scores * scores + 1.0)
    return (1.0 / inverse, scores * inverse, inverse)


def score_grads(probs, soft_sign, inverse, grad_signed, delta):
    cubed = inverse * inverse * inverse
    return (
        soft_sign * probs * (grad_signed * soft_sign - delta[..., None])
        + probs * grad_signed * cubed
    ).astype(jnp.bfloat16)


def attend_piece(query_heads, row_pos, state, pair):
    key_rows, val_rows = pair
    seq_count, key_count = (key_rows.shape[0], key_rows.shape[1])
    head_count = query_heads.shape[2]
    key_heads = key_rows.reshape(seq_count, key_count, head_count, -1)
    val_heads = val_rows.reshape(seq_count, key_count, head_count, -1)
    scores = (
        jnp.einsum("sqhd,skhd->shqk", query_heads, key_heads, preferred_element_type=jnp.float32)
        * 0.125
    )
    soft_mag, soft_sign, inverse = smooth_parts(scores)
    key_pos = jnp.arange(key_count, dtype=jnp.int32)
    allowed = key_pos[None, :] <= row_pos[:, None]
    magnitude = jnp.where(allowed, soft_mag, -1e30)
    old_max, denom, acc_low, acc_rest = state
    new_max = jnp.maximum(old_max, jnp.max(magnitude, axis=-1))
    weights = jnp.where(allowed, jnp.exp(magnitude - new_max[..., None]), 0.0)
    signed = weights * soft_sign
    signed_low = signed.astype(jnp.bfloat16)
    signed_rest = (signed - signed_low.astype(jnp.float32)).astype(jnp.bfloat16)
    rescale = jnp.exp(old_max - new_max)
    denom = jnp.sum(weights, axis=-1)
    factor = jnp.swapaxes(rescale, 1, 2)[..., None]
    acc_low = acc_low * factor + jnp.einsum(
        "shqk,skhd->sqhd", signed_low, val_heads, preferred_element_type=jnp.float32
    )
    acc_rest = acc_rest * factor + jnp.einsum(
        "shqk,skhd->sqhd", signed_rest, val_heads, preferred_element_type=jnp.float32
    )
    return (new_max, denom, acc_low, acc_rest)


def return_piece(query_heads, grad_heads, log_total, delta, row_pos, pair):
    key_rows, val_rows = pair
    seq_count, key_count, model_width = key_rows.shape
    head_count = query_heads.shape[2]
    key_heads = key_rows.reshape(seq_count, key_count, head_count, -1)
    val_heads = val_rows.reshape(seq_count, key_count, head_count, -1)
    scores = (
        jnp.einsum("sqhd,skhd->shqk", query_heads, key_heads, preferred_element_type=jnp.float32)
        * 0.125
    )
    soft_mag, soft_sign, inverse = smooth_parts(scores)
    key_pos = jnp.arange(key_count, dtype=jnp.int32)
    allowed = key_pos[None, :] <= row_pos[:, None]
    probs = jnp.where(allowed, jnp.exp(soft_mag - log_total[..., None]), 0.0)
    signed_low = (probs * soft_sign).astype(jnp.bfloat16)
    grad_signed = jnp.einsum(
        "sqhd,skhd->shqk", grad_heads, val_heads, preferred_element_type=jnp.float32
    )
    grad_scores = score_grads(probs, soft_sign, inverse, grad_signed, delta)
    grad_query = 0.125 * jnp.einsum(
        "shqk,skhd->sqhd", grad_scores, key_heads, preferred_element_type=jnp.float32
    )
    grad_keys = 0.125 * jnp.einsum(
        "shqk,sqhd->skhd", grad_scores, query_heads, preferred_element_type=jnp.float32
    )
    grad_vals = jnp.einsum(
        "shqk,sqhd->skhd", signed_low, grad_heads, preferred_element_type=jnp.float32
    )
    both_grads = jnp.concatenate(
        [
            grad_keys.reshape(seq_count, key_count, model_width),
            grad_vals.reshape(seq_count, key_count, model_width),
        ],
        -1,
    )
    return (grad_query, both_grads)


def shards(
    tokens, seq_len, ln1_gain, ln1_shift, w_qkv, w_out, ln2_gain, ln2_shift, w_up, w_down, cotangent
):
    seqs_here, block_len, model_width = tokens.shape
    head_count = HEADS
    head_width = model_width // head_count
    row_count = seqs_here * block_len
    gathered = (
        lax.all_gather(ln1_gain, ("blk", "seq"), axis=0, tiled=True),
        lax.all_gather(ln1_shift, ("blk", "seq"), axis=0, tiled=True),
        lax.all_gather(w_qkv, ("blk", "seq"), axis=0, tiled=True),
        lax.all_gather(w_out, ("blk", "seq"), axis=0, tiled=True),
        lax.all_gather(ln2_gain, ("blk", "seq"), axis=0, tiled=True),
        lax.all_gather(ln2_shift, ("blk", "seq"), axis=0, tiled=True),
        lax.all_gather(w_up, ("blk", "seq"), axis=0, tiled=True),
        lax.all_gather(w_down, ("blk", "seq"), axis=0, tiled=True),
    )
    gain_one = gathered[0].astype(jnp.float32)
    shift_one = gathered[1].astype(jnp.float32)
    qkv_full, out_full = (gathered[2], gathered[3])
    gain_two = gathered[4].astype(jnp.float32)
    shift_two = gathered[5].astype(jnp.float32)
    up_full, down_full = (gathered[6], gathered[7])
    row_pos = lax.axis_index("blk") * block_len + jnp.arange(block_len, dtype=jnp.int32)
    live_rows = (row_pos[None, :] < seq_len[:, None]).astype(jnp.float32).reshape(row_count, 1)
    inputs = tokens.astype(jnp.float32).reshape(row_count, model_width)
    normed_low = normalize(inputs, gain_one, shift_one).astype(jnp.bfloat16)
    projected = jnp.dot(normed_low, qkv_full, preferred_element_type=jnp.float32).astype(
        jnp.bfloat16
    )
    projected = projected.reshape(seqs_here, block_len, 3 * model_width)
    queries = projected[..., :model_width]
    key_rows = projected[..., model_width : 2 * model_width]
    val_rows = projected[..., 2 * model_width :]
    query_heads = queries.reshape(seqs_here, block_len, head_count, head_width)
    acc_zero = jnp.zeros((seqs_here, block_len, head_count, head_width), jnp.float32)
    start_state = (
        jnp.full((seqs_here, head_count, block_len), -1e30, jnp.float32),
        jnp.zeros((seqs_here, head_count, block_len), jnp.float32),
        acc_zero,
        acc_zero,
    )
    run_max, denom, acc_low, acc_rest = attend_piece(
        query_heads,
        row_pos,
        start_state,
        (
            lax.all_gather(key_rows, "blk", axis=1, tiled=True),
            lax.all_gather(val_rows, "blk", axis=1, tiled=True),
        ),
    )
    denom_rows = jnp.swapaxes(denom, 1, 2)[..., None]
    attended = acc_low / denom_rows
    attended_full = (acc_low + acc_rest) / denom_rows
    log_total = run_max + jnp.log(denom)
    att_low = attended.reshape(row_count, model_width).astype(jnp.bfloat16)
    branch = jnp.dot(att_low, out_full, preferred_element_type=jnp.float32)
    middle = inputs + branch * live_rows
    normed_two_low = normalize(middle, gain_two, shift_two).astype(jnp.bfloat16)
    hidden_pre = jnp.dot(normed_two_low, up_full, preferred_element_type=jnp.float32)
    hidden_low = jax.nn.gelu(hidden_pre, approximate=True).astype(jnp.bfloat16)
    mlp_out = jnp.dot(hidden_low, down_full, preferred_element_type=jnp.float32)
    result = (middle + mlp_out).astype(jnp.bfloat16).reshape(seqs_here, block_len, model_width)
    grad_top = cotangent.reshape(row_count, model_width)
    grad_down = jnp.einsum("tf,td->fd", hidden_low, grad_top, preferred_element_type=jnp.float32)
    grad_hidden = jnp.einsum("td,fd->tf", grad_top, down_full, preferred_element_type=jnp.float32)
    gelu_pull = jax.vjp(lambda values: jax.nn.gelu(values, approximate=True), hidden_pre)[1]
    grad_pre_low = gelu_pull(grad_hidden)[0].astype(jnp.bfloat16)
    grad_up = jnp.einsum(
        "td,tf->df", normed_two_low, grad_pre_low, preferred_element_type=jnp.float32
    )
    grad_normed_two = jnp.einsum(
        "tf,df->td", grad_pre_low, up_full, preferred_element_type=jnp.float32
    )
    norm_pull_two = jax.vjp(normalize, middle, gain_two, shift_two)[1]
    grad_mid_norm, grad_gain_two, grad_shift_two = norm_pull_two(grad_normed_two)
    grad_mid = grad_top.astype(jnp.float32) + grad_mid_norm
    grad_branch_low = (grad_mid * live_rows).astype(jnp.bfloat16)
    grad_out_w = jnp.einsum(
        "td,te->de", att_low, grad_branch_low, preferred_element_type=jnp.float32
    )
    grad_att_low = jnp.einsum(
        "te,de->td", grad_branch_low, out_full, preferred_element_type=jnp.float32
    ).astype(jnp.bfloat16)
    grad_heads = grad_att_low.reshape(seqs_here, block_len, head_count, head_width)
    delta = jnp.swapaxes(jnp.sum(grad_heads.astype(jnp.float32) * attended_full, axis=-1), 1, 2)
    grad_query, grad_pairs = return_piece(
        query_heads,
        grad_heads,
        log_total,
        delta,
        row_pos,
        (
            lax.all_gather(key_rows, "blk", axis=1, tiled=True),
            lax.all_gather(val_rows, "blk", axis=1, tiled=True),
        ),
    )
    grad_pairs_own = lax.psum_scatter(
        grad_pairs.astype(jnp.bfloat16), "blk", scatter_dimension=1, tiled=True
    ).astype(jnp.float32)
    grad_query_own = grad_query.reshape(seqs_here, block_len, model_width)
    grad_qkv_low = (
        jnp.concatenate([grad_query_own, grad_pairs_own], -1)
        .astype(jnp.bfloat16)
        .reshape(row_count, 3 * model_width)
    )
    grad_qkv_w = jnp.einsum(
        "td,tf->df", normed_low, grad_qkv_low, preferred_element_type=jnp.float32
    )
    grad_normed_one = jnp.einsum(
        "tf,df->td", grad_qkv_low, qkv_full, preferred_element_type=jnp.float32
    )
    norm_pull_one = jax.vjp(normalize, inputs, gain_one, shift_one)[1]
    grad_in_norm, grad_gain_one, grad_shift_one = norm_pull_one(grad_normed_one)
    grad_input = (grad_mid + grad_in_norm).reshape(seqs_here, block_len, model_width)
    shares = (
        lax.psum_scatter(grad_gain_one, ("blk", "seq"), scatter_dimension=0, tiled=True),
        lax.psum_scatter(grad_shift_one, ("blk", "seq"), scatter_dimension=0, tiled=True),
        lax.psum_scatter(grad_qkv_w, ("blk", "seq"), scatter_dimension=0, tiled=True),
        lax.psum_scatter(grad_out_w, ("blk", "seq"), scatter_dimension=0, tiled=True),
        lax.psum_scatter(grad_gain_two, ("blk", "seq"), scatter_dimension=0, tiled=True),
        lax.psum_scatter(grad_shift_two, ("blk", "seq"), scatter_dimension=0, tiled=True),
        lax.psum_scatter(grad_up, ("blk", "seq"), scatter_dimension=0, tiled=True),
        lax.psum_scatter(grad_down, ("blk", "seq"), scatter_dimension=0, tiled=True),
    )
    return (
        result,
        grad_input,
        shares[0],
        shares[1],
        shares[2],
        shares[3],
        shares[4],
        shares[5],
        shares[6],
        shares[7],
    )


def solution(mesh):
    return jax.shard_map(
        shards,
        mesh=mesh,
        in_specs=(
            P("seq", "blk", None),
            P("seq"),
            P(("blk", "seq")),
            P(("blk", "seq")),
            P(("blk", "seq"), None),
            P(("blk", "seq"), None),
            P(("blk", "seq")),
            P(("blk", "seq")),
            P(("blk", "seq"), None),
            P(("blk", "seq"), None),
            P("seq", "blk", None),
        ),
        out_specs=(
            P("seq", "blk", None),
            P("seq", "blk", None),
            P(("blk", "seq")),
            P(("blk", "seq")),
            P(("blk", "seq"), None),
            P(("blk", "seq"), None),
            P(("blk", "seq")),
            P(("blk", "seq")),
            P(("blk", "seq"), None),
            P(("blk", "seq"), None),
        ),
        check_vma=False,
    )
```

profile of v0, /device:TPU:0, one launch (start us, length us, event | category | flops | bytes accessed | tf_op | source)
XLA Modules:
  0.0 1339.2 jit_solution(3102794879292885736)
XLA Ops:
  11.3 42.2 %all-reduce.9 = (bf16[768]{0:T(1024)(128)(2,1)S(1)}, bf16[768]{0:T(1024)(128)(2,1)S(1)}, bf16[768]{0:T(1024)(128)(2,1)S(1)}, bf16[768]{0:T(1024)(128)(2,1)S(1)}) all-reduce(bf16[768]{0:T(1024)(128)(2,1)S(1)} %dynamic-update-slice.1, bf16[768]{0:T(1024)(128)(2,1)S(1)} %dynamic-update-slice, ...), channel_id=1, replica_groups=mesh['blk'=4,'seq'=8] {'blk','seq'}, use_global_device_ids=true, to_apply=%add.1 | all-reduce | flops 3072 | bytes 12288
  60.5 13.5 %all-gather.7.cloned.1.call-done = bf16[768,2304]{1,0:T(8,128)(2,1)} async-done(((bf16[24,2304]{1,0:T(8,128)(2,1)}), bf16[768,2304]{1,0:T(8,128)(2,1)}) %all-gather.7.cloned.1.call-update) | async-done | bytes 3538960 | tf_op jit(solution)/shard_map/all_gather | solution.py:109
  89.0 62.2 %all-gather.9.cloned.1.call-done = bf16[2,2048,768]{2,1,0:T(8,128)(2,1)} async-done(((bf16[2,512,768]{2,1,0:T(8,128)(2,1)}), bf16[2,2048,768]{2,1,0:T(8,128)(2,1)}) %all-gather.9.cloned.1.call-update) | async-done | bytes 6291472 | tf_op jit(solution)/shard_map/all_gather | solution.py:146
  159.9 44.8 %select_reduce_fusion = (f32[2,12,512]{2,1,0:T(8,128)S(1)}, f32[2,12,512,2048]{3,2,1,0:T(8,128)}) fusion(pred[512,2048]{1,0:T(8,128)(4,1)S(1)} %copy-done.12, bf16[2,512,12,64]{1,3,2,0:T(8,128)(2,1)S(1)} %bitcast.130, bf16[2,2048,12,64]{1,3,2,0:T(8,128)(2,1)} %bitcast.118), kind=kOutput, calls=%fused_computation.13 | convolution fusion | flops 3372208128 | bytes 109625344 | tf_op jit(solution)/shard_map/sqhd,skhd->shqk/dot_general | solution.py:36
  204.7 47.1 %fusion.8 = f32[2,12,512]{2,1,0:T(8,128)S(1)} fusion(f32[2,12,512]{2,1,0:T(8,128)S(1)} %broadcast_maximum_fusion, pred[512,2048]{1,0:T(8,128)(4,1)S(1)} %copy-done.12, f32[2,12,512,2048]{3,2,1,0:T(8,128)} %get-tuple-element.35), kind=kLoop, calls=%fused_computation.14 | loop fusion | flops 201314304 | bytes 101810176 | tf_op jit(solution)/shard_map/reduce_sum | solution.py:50
  261.2 55.2 %divide_convert_fusion = (bf16[2,512,12,64]{1,3,2,0:T(8,128)(2,1)S(1)}, f32[2,12,64,512]{3,2,1,0:T(8,128)}) fusion(f32[2,512,12]{1,2,0:T(8,128)S(1)} %bitcast.136, f32[2,512,12]{1,2,0:T(8,128)S(1)} %get-tuple-element.31, bf16[2,2048,12,64]{1,3,2,0:T(8,128)(2,1)} %bitcast.121, f32[2,12,512,2048]{3,2,1,0:T(8,128)} %get-tuple-element.35, ...), kind=kOutput, calls=%fused_computation.68 | convolution fusion | flops 3475243008 | bytes 112869376 | tf_op jit(solution)/shard_map/shqk,skhd->sqhd/dot_general | solution.py:52
  324.2 22.2 %all-gather.15.cloned.1.call-done = bf16[768,3072]{1,0:T(8,128)(2,1)} async-done(((bf16[24,3072]{1,0:T(8,128)(2,1)}), bf16[768,3072]{1,0:T(8,128)(2,1)}) %all-gather.15.cloned.1.call-update) | async-done | bytes 4718608 | tf_op jit(solution)/shard_map/all_gather | solution.py:113
  346.4 11.4 fusion.56
  357.8 54.0 %all-gather.17.cloned.1.call-done = bf16[3072,768]{1,0:T(8,128)(2,1)} async-done(((bf16[96,768]{1,0:T(8,128)(2,1)}), bf16[3072,768]{1,0:T(8,128)(2,1)}) %all-gather.17.cloned.1.call-update) | async-done | bytes 4718608 | tf_op jit(solution)/shard_map/all_gather | solution.py:114
  411.8 14.0 %fusion.22 = bf16[1024,3072]{1,0:T(8,128)(2,1)S(1)} fusion(f32[1024,3072]{1,0:T(8,128)} %fusion.56, bf16[1024,768]{1,0:T(8,128)(2,1)S(1)} %bitcast.128, bf16[3072,768]{1,0:T(8,128)(2,1)} %all-gather.17.cloned.1.call-done), kind=kOutput, calls=%fused_computation.29 | convolution fusion | flops 4894752768 | bytes 25165824 | tf_op jit(solution)/shard_map/td,fd->tf/dot_general | solution.py:164
  448.5 59.6 %fusion.40 = f32[2,512,12]{1,2,0:T(8,128)} fusion(f32[2,12,64,512]{3,2,1,0:T(8,128)} %get-tuple-element.37, bf16[2,2048,12,64]{1,3,2,0:T(8,128)(2,1)} %bitcast.122, f32[2,512,12]{1,2,0:T(8,128)S(1)} %bitcast.137, f32[2,512,12]{1,2,0:T(8,128)S(1)} %get-tuple-element.31, bf16[2,512,12,64]{1,0,3,2:T(2,128)(2,1)} %reshape.195, ...), kind=kOutput, calls=%fused_computation.69 | convolution fusion | flops 3553873920 | bytes 112918528 | tf_op jit(solution)/shard_map/shqk,skhd->sqhd/dot_general | solution.py:55
  508.1 56.0 %fusion.23 = bf16[2,12,64,2048]{3,2,1,0:T(8,128)(2,1)} fusion(f32[2,12,512,2048]{3,2,1,0:T(8,128)} %get-tuple-element.35, f32[2,12,512]{2,1,0:T(8,128)S(1)} %copy-done.33, pred[512,2048]{1,0:T(8,128)(4,1)S(1)} %copy-done.13, bf16[2,512,12,64]{1,0,3,2:T(2,128)(2,1)S(1)} %copy-done.17), kind=kOutput, calls=%fused_computation.37 | convolution fusion | flops 3450863616 | bytes 109625344 | tf_op jit(solution)/shard_map/shqk,sqhd->skhd/dot_general | solution.py:86
  564.1 86.4 %fusion.2 = bf16[2,12,512,2048]{3,2,1,0:T(8,128)(2,1)} fusion(f32[2,12,512,2048]{3,2,1,0:T(8,128)} %get-tuple-element.35, f32[2,12,512]{2,1,0:T(8,128)S(1)} %bitcast.149, f32[2,12,512]{2,1,0:T(8,128)S(1)} %copy-done.33, pred[512,2048]{1,0:T(8,128)(4,1)S(1)} %copy-done.13, bf16[2,2048,12,64]{1,3,2,0:T(8,128)(2,1)} %bitcast.123, ...), kind=kOutput, calls=%fused_computation.3 | convolution fusion | flops 3649044480 | bytes 160006144 | tf_op jit(solution)/shard_map/sqhd,skhd->shqk/dot_general | solution.py:76
  650.5 21.5 %multiply_convert_fusion = bf16[2,12,64,2048]{3,2,1,0:T(8,128)(2,1)} fusion(bf16[2,512,12,64]{1,3,2,0:T(8,128)(2,1)S(1)} %bitcast.131, bf16[2,12,512,2048]{3,2,1,0:T(8,128)(2,1)} %fusion.2), kind=kOutput, calls=%fused_computation.31 | convolution fusion | flops 3227516928 | bytes 58195968 | tf_op jit(solution)/shard_map/shqk,sqhd->skhd/dot_general | solution.py:83
  704.6 11.4 fusion.55
  717.4 12.5 fusion.57
  730.0 23.7 %fusion.43 = bf16[2,512,12,64]{1,3,2,0:T(8,128)(2,1)S(1)} fusion(bf16[2,2048,12,64]{1,3,2,0:T(8,128)(2,1)} %bitcast.119, bf16[2,12,512,2048]{3,2,1,0:T(8,128)(2,1)} %fusion.2), kind=kOutput, calls=%fused_computation.73 | convolution fusion | flops 3222798336 | bytes 58195968 | tf_op jit(solution)/shard_map/shqk,skhd->sqhd/dot_general | solution.py:80
  757.2 62.0 %reduce-scatter.6.cloned.1.call-done = bf16[2,512,1536]{2,1,0:T(8,128)(2,1)} async-done(((bf16[2,2048,1536]{2,1,0:T(8,128)(2,1)}), bf16[2,512,1536]{2,1,0:T(8,128)(2,1)}) %reduce-scatter.6.cloned.1.call-update) | async-done | bytes 3145744 | tf_op jit(solution)/shard_map/reduce_scatter | solution.py:196
  829.0 13.5 %add_convert_fusion = bf16[1024,768]{1,0:T(8,128)(2,1)} fusion(f32[1024,768]{1,0:T(8,128)} %copy-done.2, bf16[3072,768]{1,0:T(8,128)(2,1)} %all-gather.17.cloned.1.call-done, f32[1024,3072]{1,0:T(8,128)} %fusion.56), kind=kOutput, calls=%fused_computation.65 | convolution fusion | flops 4861722624 | bytes 22020096 | tf_op jit(solution)/shard_map/dot_general | solution.py:160
  850.0 39.6 %all-reduce.8 = (f32[768]{0:T(1024)S(1)}, f32[768]{0:T(1024)S(1)}, f32[768]{0:T(1024)S(1)}, f32[768]{0:T(1024)S(1)}) all-reduce(f32[768]{0:T(1024)S(1)} %get-tuple-element.12, f32[768]{0:T(1024)S(1)} %get-tuple-element.15, f32[768]{0:T(1024)S(1)} %copy-done.39, ...), channel_id=3, replica_groups=mesh['blk'=4,'seq'=8] {'blk','seq'}, use_global_device_ids=true, to_apply=%region_13.14.clone | all-reduce | flops 3072 | bytes 24576
  896.8 27.4 %reduce-scatter.10.cloned.1.call-done = f32[24,768]{1,0:T(8,128)} async-done(((f32[768,768]{1,0:T(8,128)}), f32[24,768]{1,0:T(8,128)}) %reduce-scatter.10.cloned.1.call-update) | async-done | bytes 73744 | tf_op jit(solution)/shard_map/reduce_scatter | solution.py:218
  924.3 142.0 %reduce-scatter.12.cloned.1.call-done = f32[24,3072]{1,0:T(8,128)} async-done(((f32[768,3072]{1,0:T(8,128)}), f32[24,3072]{1,0:T(8,128)}) %reduce-scatter.12.cloned.1.call-update) | async-done | bytes 294928 | tf_op jit(solution)/shard_map/reduce_scatter | solution.py:221
  1066.3 141.0 %reduce-scatter.14.cloned.1.call-done = f32[96,768]{1,0:T(8,128)} async-done(((f32[3072,768]{1,0:T(8,128)}), f32[96,768]{1,0:T(8,128)}) %reduce-scatter.14.cloned.1.call-update) | async-done | bytes 294928 | tf_op jit(solution)/shard_map/reduce_scatter | solution.py:222
  1207.3 125.1 %reduce-scatter.8.cloned.1.call-done = f32[24,2304]{1,0:T(8,128)} async-done(((f32[768,2304]{1,0:T(8,128)}), f32[24,2304]{1,0:T(8,128)}) %reduce-scatter.8.cloned.1.call-update) | async-done | bytes 221200 | tf_op jit(solution)/shard_map/reduce_scatter | solution.py:217
  (178 shorter events, 136.1 us)
Async XLA Ops:
  7.2 66.8 %all-gather.7.cloned.1.call-start = ((), (), s32[]{:S(2)}) async-start(), calls=%async_computation.5 | async-start | bytes 3649536 | tf_op jit(solution)/shard_map/all_gather | solution.py:109
  7.9 143.2 %all-gather.9.cloned.1.call-start = ((), (), s32[]{:S(2)}) async-start(), calls=%async_computation.6 | async-start | bytes 7864320 | tf_op jit(solution)/shard_map/all_gather | solution.py:146
  60.5 19.6 %copy-start.14 = (bf16[1024,768]{1,0:T(8,128)(2,1)}, bf16[1024,768]{1,0:T(8,128)(2,1)S(1)}, u32[]{:S(2)}) copy-start(bf16[1024,768]{1,0:T(8,128)(2,1)S(1)} %fusion.35) | copy-start | bytes 4718596
  82.0 170.4 %all-gather.11.cloned.1.call-start = ((), (), s32[]{:S(2)}) async-start(), calls=%async_computation.7 | async-start | bytes 7864320 | tf_op jit(solution)/shard_map/all_gather | solution.py:147
  82.8 235.6 %all-gather.13.cloned.1.call-start = ((), (), s32[]{:S(2)}) async-start(), calls=%async_computation.8 | async-start | bytes 1216512 | tf_op jit(solution)/shard_map/all_gather | solution.py:110
  83.4 263.0 %all-gather.15.cloned.1.call-start = ((), (), s32[]{:S(2)}) async-start(), calls=%async_computation.9 | async-start | bytes 4866048 | tf_op jit(solution)/shard_map/all_gather | solution.py:113
  83.9 327.8 %all-gather.17.cloned.1.call-start = ((), (), s32[]{:S(2)}) async-start(), calls=%async_computation.10 | async-start | bytes 4866048 | tf_op jit(solution)/shard_map/all_gather | solution.py:114
  84.5 734.8 %reduce-scatter.6.cloned.1.call-start = ((), (), s32[]{:S(2)}) async-start(), calls=%async_computation.11 | async-start | bytes 15728640 | tf_op jit(solution)/shard_map/reduce_scatter | solution.py:196
  89.0 70.9 %copy-start.10 = (bf16[2,512,768]{1,2,0:T(8,128)(2,1)}, bf16[2,512,768]{1,2,0:T(8,128)(2,1)S(1)}, u32[]{:S(2)}) copy-start(bf16[2,512,768]{1,2,0:T(8,128)(2,1)S(1)} %copy.36) | copy-start | bytes 4718596
  89.0 70.9 %copy-start.12 = (pred[512,2048]{1,0:T(8,128)(4,1)S(1)}, pred[512,2048]{1,0:T(8,128)(4,1)}, u32[]{:S(2)}) copy-start(pred[512,2048]{1,0:T(8,128)(4,1)} %iota_compare_fusion) | copy-start | bytes 3145732
  318.4 28.0 %copy-start.23 = (f32[768]{0:T(1024)S(1)}, f32[768]{0:T(1024)}, u32[]{:S(2)}) copy-start(f32[768]{0:T(1024)} %convert_element_type.90) | copy-start | bytes 9220
  318.5 27.9 %copy-start.31 = (f32[768]{0:T(1024)S(1)}, f32[768]{0:T(1024)}, u32[]{:S(2)}) copy-start(f32[768]{0:T(1024)} %convert_element_type.91) | copy-start | bytes 9220
  322.0 114.7 %copy-start.19 = (f32[1024]{0:T(1024)}, f32[1024]{0:T(1024)S(1)}, u32[]{:S(2)}) copy-start(f32[1024]{0:T(1024)S(1)} %broadcast_multiply_fusion) | copy-start | bytes 12292
  324.2 112.5 %copy-start.21 = (f32[1024]{0:T(1024)}, f32[1024]{0:T(1024)S(1)}, u32[]{:S(2)}) copy-start(f32[1024]{0:T(1024)S(1)} %fusion.47) | copy-start | bytes 12292
  324.2 87.6 %copy-start.8 = (bf16[2,512,768]{2,1,0:T(8,128)(2,1)S(1)}, bf16[2,512,768]{2,1,0:T(8,128)(2,1)}, u32[]{:S(2)}) copy-start(bf16[2,512,768]{2,1,0:T(8,128)(2,1)} %param.21) | copy-start | bytes 4718596
  448.5 59.6 %copy-start.17 = (bf16[2,512,12,64]{1,0,3,2:T(2,128)(2,1)S(1)}, bf16[2,512,12,64]{1,0,3,2:T(2,128)(2,1)}, u32[]{:S(2)}) copy-start(bf16[2,512,12,64]{1,0,3,2:T(2,128)(2,1)} %reshape.195) | copy-start | bytes 4718596
  448.5 59.6 %copy-start.33 = (f32[2,12,512]{2,1,0:T(8,128)S(1)}, f32[2,12,512]{2,1,0:T(8,128)}, u32[]{:S(2)}) copy-start(f32[2,12,512]{2,1,0:T(8,128)} %get-tuple-element.30) | copy-start | bytes 147460
  508.1 56.0 %copy-start.45 = (f32[2,512,12]{1,2,0:T(8,128)S(1)}, f32[2,512,12]{1,2,0:T(8,128)}, u32[]{:S(2)}) copy-start(f32[2,512,12]{1,2,0:T(8,128)} %fusion.40) | copy-start | bytes 147460
  564.1 86.4 %copy-start.11 = (bf16[2,512,768]{1,2,0:T(8,128)(2,1)S(1)}, bf16[2,512,768]{1,2,0:T(8,128)(2,1)}, u32[]{:S(2)}) copy-start(bf16[2,512,768]{1,2,0:T(8,128)(2,1)} %copy-done.10) | copy-start | bytes 4718596
  699.6 224.7 %reduce-scatter.10.cloned.1.call-start = ((), (), s32[]{:S(2)}) async-start(), calls=%async_computation.13 | async-start | bytes 2433024 | tf_op jit(solution)/shard_map/reduce_scatter | solution.py:218
  704.5 361.8 %reduce-scatter.12.cloned.1.call-start = ((), (), s32[]{:S(2)}) async-start(), calls=%async_computation.14 | async-start | bytes 9732096 | tf_op jit(solution)/shard_map/reduce_scatter | solution.py:221
  716.0 491.3 %reduce-scatter.14.cloned.1.call-start = ((), (), s32[]{:S(2)}) async-start(), calls=%async_computation.15 | async-start | bytes 9732096 | tf_op jit(solution)/shard_map/reduce_scatter | solution.py:222
  729.9 602.5 %reduce-scatter.8.cloned.1.call-start = ((), (), s32[]{:S(2)}) async-start(), calls=%async_computation.12 | async-start | bytes 7299072 | tf_op jit(solution)/shard_map/reduce_scatter | solution.py:217
  846.7 45.3 %copy-start.35 = (f32[1024]{0:T(1024)S(1)}, f32[1024]{0:T(1024)}, u32[]{:S(2)}) copy-start(f32[1024]{0:T(1024)} %copy-done.34) | copy-start | bytes 12292
  (33 other events, 192.6 us)
Sparse Core Ops, SparseCore 0:
  11.0 62.9 all-gather.6
  82.2 68.9 all-gather.8
  153.6 70.1 all-gather.10
  226.7 54.2 all-gather.12
  283.8 62.5 all-gather.14
  349.3 62.4 all-gather.16
  699.7 119.5 reduce-scatter.5
  825.2 99.0 reduce-scatter.9
  931.7 134.5 reduce-scatter.11
  1072.6 134.6 reduce-scatter.13
  1214.5 117.8 reduce-scatter.7
where the time goes:
time: 1340 us
  waiting for transfers between devices  653 us (49%)
  matrix products  451 us (34%)
  blocking collectives  81.8 us (6%)
  other arithmetic  75.9 us (6%)
  local copies, waits for them, and re-layouts  62.2 us (5%)
  between operations  14.8 us (1%)
    reduce_scatter x1, waiting for transfers between devices, shards(): lax.psum_scatter(grad_up, ('blk', 'seq'), scatter_dimension=0, tiled=True)  142 us
    reduce_scatter x1, waiting for transfers between devices, shards(): lax.psum_scatter(grad_down, ('blk', 'seq'), scatter_dimension=0, tiled=True)  141 us
    reduce_scatter x1, waiting for transfers between devices, shards(): lax.psum_scatter(grad_qkv_w, ('blk', 'seq'), scatter_dimension=0, tiled=T...  125 us
    dot_general x1, matrix products, return_piece(): jnp.einsum('sqhd,skhd->shqk', grad_heads, val_heads, preferred_element_ty...  86.4 us
    unnamed x2, blocking collectives  81.8 us
    all_gather x1, waiting for transfers between devices, shards(): lax.all_gather(key_rows, 'blk', axis=1, tiled=True)  62.2 us
    reduce_scatter x1, waiting for transfers between devices, shards(): lax.psum_scatter(grad_pairs.astype(jnp.bfloat16), 'blk', scatter_dimensio...  62 us
    dot_general x1, matrix products, attend_piece(): jnp.einsum('shqk,skhd->sqhd', signed_rest, val_heads, preferred_element_t...  59.6 us
  transfers between devices with their start and end apart: 11, of which 9 were waited for; matrix products, arithmetic and copies ran while one was open for 22% of the time, Pallas kernels for 0%

commit v1 on v0

v1 whole, which is shorter than its diff:
```python
import functools

import jax
import jax.numpy as jnp
from jax import lax
from jax.experimental import pallas as pl
from jax.experimental.pallas import tpu as pltpu
from jax.sharding import PartitionSpec as P

HEADS = 12
VMEM_LIMIT = 60 * 2**20


def dot_nt(left, right):
    return lax.dot_general(left, right, (((1,), (1,)), ((), ())), preferred_element_type=jnp.float32)


def dot_nn(left, right):
    return lax.dot_general(left, right, (((1,), (0,)), ((), ())), preferred_element_type=jnp.float32)


def split_heads(dst, src):
    low = lax.broadcasted_iota(jnp.int32, src.shape, 1) < 64
    dst[0] = jnp.where(low, src, jnp.zeros_like(src))
    dst[1] = jnp.where(low, jnp.zeros_like(src), src)


def causal(bk, bq, kj, qi):
    kpos = kj * bk + lax.broadcasted_iota(jnp.int32, (bk, bq), 0)
    qpos = qi * bq + lax.broadcasted_iota(jnp.int32, (bk, bq), 1)
    return kpos <= qpos


def fwd_kernel(bq, bk, q_ref, k_ref, v_ref, att_ref, lse_ref, kh, vt):
    length = q_ref.shape[0]
    split_heads(kh, k_ref[...])
    vt[...] = v_ref[...].astype(jnp.float32).T.astype(jnp.bfloat16)
    ratio = bq // bk

    def q_step(qi, _):
        q_rows = q_ref[pl.ds(pl.multiple_of(qi * bq, bq), bq), :]

        def one(kj, state, masked):
            at = pl.ds(pl.multiple_of(kj * bk, bk), bk)
            out = []
            for h in range(2):
                peak, total, acc = state[3 * h : 3 * h + 3]
                s = dot_nt(kh[h, at, :], q_rows)
                u = s * s + 1.0
                inv = lax.rsqrt(u)
                mag = u * inv
                if masked:
                    mag = jnp.where(causal(bk, bq, kj, qi), mag, -1e30)
                new = jnp.maximum(peak, jnp.max(mag, axis=0, keepdims=True))
                p = jnp.exp(mag - new)
                alpha = jnp.exp(peak - new)
                total = total * alpha + jnp.sum(p, axis=0, keepdims=True)
                signed = (p * (s * inv)).astype(jnp.bfloat16)
                acc = acc * alpha + dot_nn(vt[64 * h : 64 * h + 64, at], signed)
                out += [new, total, acc]
            return tuple(out)

        zero = (
            jnp.full((1, bq), -1e30, jnp.float32),
            jnp.zeros((1, bq), jnp.float32),
            jnp.zeros((64, bq), jnp.float32),
        )
        state = zero + zero
        for r in range(ratio):
            state = one(qi * ratio + r, state, True)
        state = lax.fori_loop(0, qi * ratio, lambda kj, st: one(kj, st, False), state)
        rows = pl.ds(pl.multiple_of(qi * bq, bq), bq)
        both = []
        for h in range(2):
            peak, total, acc = state[3 * h : 3 * h + 3]
            both.append(acc / total)
            lse_ref[0, h : h + 1, rows] = peak + jnp.log(total)
        att_ref[rows, :] = jnp.concatenate(both, 0).T.astype(jnp.bfloat16)
        return 0

    lax.fori_loop(0, length // bq, q_step, 0)


def attend(qkv, bq=256, bk=256):
    length, width = qkv.shape
    pairs = width // 384
    return pl.pallas_call(
        functools.partial(fwd_kernel, bq, bk),
        grid=(pairs,),
        out_shape=(
            jax.ShapeDtypeStruct((length, 128 * pairs), jnp.bfloat16),
            jax.ShapeDtypeStruct((pairs, 8, length), jnp.float32),
        ),
        in_specs=[pl.BlockSpec((length, 128), lambda p, n=n: (0, n * pairs + p)) for n in range(3)],
        out_specs=(
            pl.BlockSpec((length, 128), lambda p: (0, p)),
            pl.BlockSpec((1, 8, length), lambda p: (p, 0, 0)),
        ),
        scratch_shapes=[
            pltpu.VMEM((2, length, 128), jnp.bfloat16),
            pltpu.VMEM((128, length), jnp.bfloat16),
        ],
        compiler_params=pltpu.CompilerParams(vmem_limit_bytes=VMEM_LIMIT),
    )(qkv, qkv, qkv)


def bwd_kernel(bq, bk, pairs, q_ref, k_ref, v_ref, g_ref, att_ref, lse_ref, out_ref, kh, vh, qh, gh, kt, delta, dqt, dk, dv):
    pair = pl.program_id(0)
    length = q_ref.shape[0]
    width = 128 * pairs
    split_heads(kh, k_ref[...])
    split_heads(vh, v_ref[...])
    split_heads(qh, q_ref[...])
    split_heads(gh, g_ref[...])
    kt[...] = k_ref[...].astype(jnp.float32).T.astype(jnp.bfloat16)
    prod = (g_ref[...].astype(jnp.float32) * att_ref[...].astype(jnp.float32)).T
    delta[0:1, :] = jnp.sum(prod[:64], axis=0, keepdims=True)
    delta[1:2, :] = jnp.sum(prod[64:], axis=0, keepdims=True)
    dqt[...] = jnp.zeros_like(dqt)

    def k_step(kj, _):
        at = pl.ds(pl.multiple_of(kj * bk, bk), bk)

        def one(qi, masked):
            rows = pl.ds(pl.multiple_of(qi * bq, bq), bq)
            q_rows = q_ref[rows, :]
            g_rows = g_ref[rows, :]
            add_k = add_v = None
            for h in range(2):
                s = dot_nt(kh[h, at, :], q_rows)
                dp = dot_nt(vh[h, at, :], g_rows)
                u = s * s + 1.0
                inv = lax.rsqrt(u)
                arg = u * inv - lse_ref[0, h : h + 1, rows]
                if masked:
                    arg = jnp.where(causal(bk, bq, kj, qi), arg, -1e30)
                p = jnp.exp(arg)
                sgn = s * inv
                t = inv * inv * (inv - 1.0) + 1.0
                ds = (p * (dp * t - sgn * delta[h : h + 1, rows])).astype(jnp.bfloat16)
                signed = (p * sgn).astype(jnp.bfloat16)
                one_v = dot_nn(signed, gh[h, rows, :])
                one_k = dot_nn(ds, qh[h, rows, :])
                add_v = one_v if h == 0 else add_v + one_v
                add_k = one_k if h == 0 else add_k + one_k
                dqt[64 * h : 64 * h + 64, rows] += dot_nn(kt[64 * h : 64 * h + 64, at], ds)
            return add_k, add_v

        first = one(kj, True)
        dk[...], dv[...] = first

        def more(qi, _):
            add_k, add_v = one(qi, False)
            dk[...] += add_k
            dv[...] += add_v
            return 0

        lax.fori_loop(kj + 1, length // bq, more, 0)
        out_ref[at, pl.ds(pl.multiple_of(width + pair * 128, 128), 128)] = dk[...].astype(jnp.bfloat16)
        out_ref[at, pl.ds(pl.multiple_of(2 * width + pair * 128, 128), 128)] = dv[...].astype(jnp.bfloat16)
        return 0

    lax.fori_loop(0, length // bk, k_step, 0)
    out_ref[:, pl.ds(pl.multiple_of(pair * 128, 128), 128)] = (dqt[...] * 0.125).T.astype(jnp.bfloat16)


def attend_back(qkv, g_att, att, lse, bq=256, bk=256):
    length, width = qkv.shape
    pairs = width // 384
    return pl.pallas_call(
        functools.partial(bwd_kernel, bq, bk, pairs),
        grid=(pairs,),
        out_shape=jax.ShapeDtypeStruct((length, width), jnp.bfloat16),
        in_specs=[pl.BlockSpec((length, 128), lambda p, n=n: (0, n * pairs + p)) for n in range(3)]
        + [pl.BlockSpec((length, 128), lambda p: (0, p))] * 2
        + [pl.BlockSpec((1, 8, length), lambda p: (p, 0, 0))],
        out_specs=pl.BlockSpec((length, width), lambda p: (0, 0)),
        scratch_shapes=[pltpu.VMEM((2, length, 128), jnp.bfloat16)] * 4
        + [
            pltpu.VMEM((128, length), jnp.bfloat16),
            pltpu.VMEM((8, length), jnp.float32),
            pltpu.VMEM((128, length), jnp.float32),
            pltpu.VMEM((bk, 128), jnp.float32),
            pltpu.VMEM((bk, 128), jnp.float32),
        ],
        compiler_params=pltpu.CompilerParams(vmem_limit_bytes=VMEM_LIMIT),
    )(qkv, qkv, qkv, g_att, att, lse)


MESH = pl.DeviceIdType.MESH


class Place:
    def __init__(self, blocks, lanes, seqs):
        self.blocks, self.depth, self.seqs = blocks, lanes // 2, seqs
        self.share = blocks // seqs
        self.bits = max(1, blocks.bit_length() - 1)
        self.blk = lax.axis_index("blk")
        lane = lax.axis_index("seq")
        self.z, self.core = lane // 2, lane % 2
        flat = self.blk * 2 + self.core
        self.seq, self.part = flat // self.share, flat % self.share

    def at(self, blk, z, core):
        return (blk, z * 2 + core)

    def bit(self, part, step):
        return 1 << ((part + step) % self.bits)


def greet(devices):
    barrier = pltpu.get_barrier_semaphore()
    for device in devices:
        pl.semaphore_signal(barrier, inc=1, device_id=device, device_id_type=MESH)
    pl.semaphore_wait(barrier, len(devices))


def send(src, dst, send_sem, recv_sem, device):
    copy = pltpu.make_async_remote_copy(
        src_ref=src, dst_ref=dst, send_sem=send_sem, recv_sem=recv_sem, device_id=device, device_id_type=MESH
    )
    copy.start()
    return copy


def arrived(ref, sem):
    pltpu.make_async_copy(ref, ref, sem).wait()


def gather_kernel(sizes, shapes, *refs):
    place = Place(*sizes)
    blocks, depth, seqs, share, bits = place.blocks, place.depth, place.seqs, place.share, place.bits
    count = len(shapes)
    tok, cot = refs[0], refs[1]
    shards = refs[2 : 2 + count]
    refs = refs[2 + count :]
    tok_all, cot_own = refs[0], refs[1]
    fulls = refs[2 : 2 + count]
    cols = refs[2 + count]
    tok_s, tok_r, near_s, near_r, cot_s, cot_r, z_s, z_r, b_s, b_r, c_s, c_r, loc = refs[3 + count :]
    blk, z, core, seq, part = place.blk, place.z, place.core, place.seq, place.part
    per_seq = share // 2
    per_part = blocks // share
    sibling = place.at(blk, z, 1 - core)
    peers = [place.at(blk, lax.rem(z + k, depth), core) for k in range(1, depth)]
    for m in range(1, blocks):
        peers += [place.at(blk ^ m, z, 0), place.at(blk ^ m, z, 1)]
    greet(peers + [sibling])

    copies = []
    local = []
    home_core = seq // seqs
    for i in range(seqs):
        for h in range(per_seq):
            target = (core * seqs + i) * per_seq + h

            def away(i=i, h=h, target=target):
                send(tok.at[i], tok_all.at[blk], tok_s.at[i * per_seq + h], tok_r.at[blk], place.at(target, z, core))

            def here(i=i):
                pltpu.make_async_copy(tok.at[i], tok_all.at[blk], loc.at[0]).start()

            pl.when(target != blk)(away)
            pl.when(target == blk)(here)
    for a in range(count):
        full, shard = fulls[a], shards[a]
        for k in range(1, depth):
            copies.append(
                send(shard, full.at[blk, z, core], z_s.at[a, k - 1], z_r.at[a, k - 1], place.at(blk, lax.rem(z + k, depth), core))
            )
        own = pltpu.make_async_copy(shard, full.at[blk, z, core], loc.at[1 + a])
        own.start()
        local.append(own)

    def level(k):
        return lax.rem(z + depth - k, depth)

    def spans(k):
        masks, out, seen = [0], [], 0
        for t in range(bits):
            bit = place.bit(k, t)
            out.append((bit, list(masks), seen))
            seen += len(masks)
            masks += [m ^ bit for m in masks]
        return out

    def forward(a, k, t):
        bit, masks, seen = spans(k)[t]
        for n, m in enumerate(masks):
            src = shards[a] if (m == 0 and k == 0) else fulls[a].at[blk ^ m, level(k), core]
            copies.append(
                send(
                    src,
                    fulls[a].at[blk ^ m, level(k), core],
                    b_s.at[a, k, seen + n],
                    b_r.at[a, k, seen + n],
                    place.at(blk ^ bit, z, core),
                )
            )

    def received(a, k, t):
        bit, masks, seen = spans(k)[t]
        for n, m in enumerate(masks):
            arrived(fulls[a].at[blk ^ bit ^ m, level(k), core], b_r.at[a, k, seen + n])

    for a in range(count):
        forward(a, 0, 0)
    for i in range(seqs):
        owner = (core * seqs + i) * share + blk // per_part
        slot = lax.rem(blk, per_part)

        def away(i=i, owner=owner, slot=slot):
            send(cot.at[i], cot_own.at[slot], cot_s.at[i], cot_r.at[slot], place.at(owner // 2, z, owner % 2))

        def here(i=i, slot=slot):
            pltpu.make_async_copy(cot.at[i], cot_own.at[slot], loc.at[1 + count]).start()

        pl.when(owner != blk * 2 + core)(away)
        pl.when(owner == blk * 2 + core)(here)

    for a in range(count):
        for k in range(1, depth):
            arrived(fulls[a].at[blk, level(k), core], z_r.at[a, k - 1])
            forward(a, k, 0)
    @pl.when(core == home_core)
    def _():
        for p in range(blocks):
            @pl.when(p != blk)
            def _():
                arrived(tok_all.at[p], tok_r.at[p])

            @pl.when(p == blk)
            def _():
                arrived(tok_all.at[p], loc.at[0])

            send(tok_all.at[p], tok_all.at[p], near_s.at[p], near_r.at[p], sibling)
        for p in range(blocks):
            arrived(tok_all.at[p], near_s.at[p])

    @pl.when(core != home_core)
    def _():
        for p in range(blocks):
            arrived(tok_all.at[p], near_r.at[p])

    for own in local:
        own.wait()
    group = lax.rem(blk * 2 + 1 - core, share)
    for a in range(count):
        for t in range(bits):
            for k in range(depth):
                received(a, k, t)
                if t + 1 < bits:
                    forward(a, k, t + 1)
                elif a == 0:
                    copies.append(
                        send(
                            fulls[0].at[:, level(k), core, group],
                            cols.at[:, level(k), core],
                            c_s.at[a, k],
                            c_r.at[a, k],
                            sibling,
                        )
                    )
                    keep = pltpu.make_async_copy(
                        fulls[0].at[:, level(k), core, part], cols.at[:, level(k), core], loc.at[2 + count + k]
                    )
                    keep.start()
                    local.append(keep)
                else:
                    held = fulls[a].at[:, level(k), core]
                    copies.append(send(held, held, c_s.at[a, k], c_r.at[a, k], sibling))
    for a in range(count):
        for k in range(depth):
            if a == 0:
                arrived(cols.at[:, level(k), 1 - core], c_r.at[a, k])
            else:
                arrived(fulls[a].at[:, level(k), 1 - core], c_r.at[a, k])
    for keep in local[count:]:
        keep.wait()
    for copy in copies:
        copy.wait_send()
    for i in range(seqs):
        for h in range(per_seq):
            target = (core * seqs + i) * per_seq + h

            @pl.when(target != blk)
            def _(i=i, h=h):
                arrived(tok.at[i], tok_s.at[i * per_seq + h])

            @pl.when((target == blk) & (core != home_core))
            def _():
                arrived(tok_all.at[blk], loc.at[0])

        owner = (core * seqs + i) * share + blk // per_part

        @pl.when(owner != blk * 2 + core)
        def _(i=i):
            arrived(cot.at[i], cot_s.at[i])

    for t in range(per_part):
        source = part * per_part + t
        mine = (source == blk) & (home_core == core)

        @pl.when(mine)
        def _(t=t):
            arrived(cot_own.at[t], loc.at[1 + count])

        @pl.when(jnp.logical_not(mine))
        def _(t=t):
            arrived(cot_own.at[t], cot_r.at[t])


def gather(sizes, tok, cot, shards):
    blocks, lanes, seqs = sizes
    depth, share = lanes // 2, blocks // seqs
    count = len(shards)
    rows, width = tok.shape[1:]
    any_space = pl.BlockSpec(memory_space=pl.ANY)
    outs = [
        jax.ShapeDtypeStruct((blocks, rows, width), tok.dtype),
        jax.ShapeDtypeStruct((blocks // share, rows, width), cot.dtype),
    ]
    outs += [jax.ShapeDtypeStruct((blocks, depth, 2) + s.shape, s.dtype) for s in shards]
    outs += [jax.ShapeDtypeStruct((blocks, depth, 2) + shards[0].shape[1:], shards[0].dtype)]
    sem = pltpu.SemaphoreType.DMA
    return pl.pallas_call(
        functools.partial(gather_kernel, sizes, [s.shape for s in shards]),
        out_shape=outs,
        in_specs=[any_space] * (2 + count),
        out_specs=[any_space] * len(outs),
        scratch_shapes=[
            sem((seqs * share // 2,)),
            sem((blocks,)),
            sem((blocks,)),
            sem((blocks,)),
            sem((seqs,)),
            sem((blocks // share,)),
            sem((count, depth - 1)),
            sem((count, depth - 1)),
            sem((count, depth, blocks - 1)),
            sem((count, depth, blocks - 1)),
            sem((count, depth)),
            sem((count, depth)),
            sem((2 + count + depth,)),
        ],
        compiler_params=pltpu.CompilerParams(collective_id=0, has_side_effects=True, vmem_limit_bytes=VMEM_LIMIT),
    )(tok, cot, *shards)


def reduce_kernel(sizes, kinds, moves, *refs):
    place = Place(*sizes)
    blocks, depth, seqs, share, bits = place.blocks, place.depth, place.seqs, place.share, place.bits
    blk, z, core, seq, part = place.blk, place.z, place.core, place.seq, place.part
    count = len(kinds)
    per_part = blocks // share
    grads, refs = refs[:count], refs[count:]
    rows_in, refs = refs[:moves], refs[moves:]
    sums, refs = refs[:count], refs[count:]
    rows_out, refs = refs[:moves], refs[moves:]
    held, refs = refs[:count], refs[count:]
    near, refs = refs[:count], refs[count:]
    wide, refs = refs[:count], refs[count:]
    tall, refs = refs[:count], refs[count:]
    m_s, m_r, z_s, z_r, b_s, b_r, c_s, c_r, loc = refs
    sibling = place.at(blk, z, 1 - core)
    peers = [place.at(blk, lax.rem(z + k, depth), core) for k in range(1, depth)]
    for m in range(1, blocks):
        peers += [place.at(blk ^ m, z, 0), place.at(blk ^ m, z, 1)]
    greet(peers + [sibling])
    order = list(range(1, depth)) + [0]
    copies, local = [], {}

    def level(k):
        return lax.rem(z + k, depth)

    other = lax.rem(blk * 2 + 1 - core, share)
    for a in range(count):
        if kinds[a] == "columns" and share > 2:
            for g in range(share):

                @pl.when((g != part) & (g != other))
                def _(a=a, g=g):
                    held[a][:, :, g] = jnp.zeros(held[a].shape[:2] + held[a].shape[3:], held[a].dtype)

    for a in range(count):
        for k in order:
            if kinds[a] == "columns":
                mine = held[a].at[:, level(k), part]
                there = held[a].at[:, level(k), part]
            else:
                mine = held[a].at[:, level(k)]
                there = near[a].at[:, level(k)]
            copies.append(send(grads[a].at[:, level(k), 1 - core], there, c_s.at[a, k], c_r.at[a, k], sibling))
            keep = pltpu.make_async_copy(grads[a].at[:, level(k), core], mine, loc.at[a, k])
            keep.start()
            local[a, k] = keep
    for j in range(moves):
        for t in range(per_part):
            source = part * per_part + t
            mine = (source == blk) & (seq // seqs == core)

            @pl.when(mine)
            def _(j=j, t=t):
                pltpu.make_async_copy(rows_in[j].at[t], rows_out[j].at[lax.rem(seq, seqs)], loc.at[count, j]).start()

            @pl.when(jnp.logical_not(mine))
            def _(j=j, t=t, source=source):
                slot = lax.rem(seq, seqs)
                send(rows_in[j].at[t], rows_out[j].at[slot], m_s.at[j, t], m_r.at[j, slot], place.at(source, z, seq // seqs))

    def spans(k):
        out, seen = [], 0
        for t in range(bits):
            bit = place.bit(k, t)
            later = [place.bit(k, u) for u in range(t + 1, bits)]
            masks = [0]
            for other in later:
                masks += [m ^ other for m in masks]
            out.append((bit, masks, seen))
            seen += len(masks)
        return out

    def add(into, first, second):
        total = first[...].astype(jnp.float32) + second[...].astype(jnp.float32)
        into[...] = total.astype(into.dtype)

    def forward(a, k, t):
        bit, masks, seen = spans(k)[t]
        for n, m in enumerate(masks):
            copies.append(
                send(
                    held[a].at[blk ^ bit ^ m, level(k)],
                    wide[a].at[k, seen + n],
                    b_s.at[a, k, seen + n],
                    b_r.at[a, k, seen + n],
                    place.at(blk ^ bit, z, core),
                )
            )

    def received(a, k, t):
        bit, masks, seen = spans(k)[t]
        for n, m in enumerate(masks):
            arrived(wide[a].at[k, seen + n], b_r.at[a, k, seen + n])
            mine = held[a].at[blk ^ m, level(k)]
            add(mine, mine, wide[a].at[k, seen + n])

    for a in range(count):
        for k in order:
            local[a, k].wait()
            if kinds[a] == "columns":
                arrived(held[a].at[:, level(k), other], c_r.at[a, k])
            else:
                arrived(near[a].at[:, level(k)], c_r.at[a, k])

                def one(b, _):
                    mine = held[a].at[b, level(k)]
                    add(mine, mine, near[a].at[b, level(k)])
                    return 0

                lax.fori_loop(0, blocks, one, 0)
            forward(a, k, 0)
    for a in range(count):
        for t in range(bits):
            for k in order:
                received(a, k, t)
                if t + 1 < bits:
                    forward(a, k, t + 1)
                elif k > 0:
                    copies.append(
                        send(
                            held[a].at[blk, level(k)],
                            tall[a].at[k - 1],
                            z_s.at[a, k - 1],
                            z_r.at[a, k - 1],
                            place.at(blk, level(k), core),
                        )
                    )
    for a in range(count):
        total = held[a][blk, z].astype(jnp.float32)
        for k in range(1, depth):
            arrived(tall[a].at[k - 1], z_r.at[a, k - 1])
            total = total + tall[a][k - 1].astype(jnp.float32)
        sums[a][...] = total
    for copy in copies:
        copy.wait_send()
    for j in range(moves):
        for t in range(per_part):
            source = part * per_part + t
            mine = (source == blk) & (seq // seqs == core)

            @pl.when(mine)
            def _(j=j, t=t):
                arrived(rows_in[j].at[t], loc.at[count, j])

            @pl.when(jnp.logical_not(mine))
            def _(j=j, t=t):
                arrived(rows_in[j].at[t], m_s.at[j, t])

        for i in range(seqs):
            owner = (core * seqs + i) * share + blk // per_part

            @pl.when(owner != blk * 2 + core)
            def _(j=j, i=i):
                arrived(rows_out[j].at[i], m_r.at[j, i])


def reduce(sizes, grads, kinds, rows, cid):
    blocks, lanes, seqs = sizes
    depth, share = lanes // 2, blocks // seqs
    count, moves = len(grads), len(rows)
    any_space = pl.BlockSpec(memory_space=pl.ANY)
    in_vmem = pl.BlockSpec(memory_space=pltpu.VMEM)
    chunks = [((share,) if kind == "columns" else ()) + g.shape[3:] for g, kind in zip(grads, kinds)]
    types = [g.dtype for g in grads]
    sem = pltpu.SemaphoreType.DMA
    out = [jax.ShapeDtypeStruct(c, jnp.float32) for c in chunks]
    out += [jax.ShapeDtypeStruct((seqs,) + r.shape[1:], r.dtype) for r in rows]
    return pl.pallas_call(
        functools.partial(reduce_kernel, sizes, kinds, moves),
        out_shape=out,
        in_specs=[any_space] * (count + moves),
        out_specs=[in_vmem] * count + [any_space] * moves,
        scratch_shapes=[pltpu.VMEM((blocks, depth) + c, t) for c, t in zip(chunks, types)]
        + [
            pltpu.VMEM((1, 1, 8, 128) if kind == "columns" else (blocks, depth) + c, t)
            for c, t, kind in zip(chunks, types, kinds)
        ]
        + [pltpu.VMEM((depth, blocks - 1) + c, t) for c, t in zip(chunks, types)]
        + [pltpu.VMEM((depth - 1,) + c, t) for c, t in zip(chunks, types)]
        + [
            sem((max(1, moves), blocks // share)),
            sem((max(1, moves), seqs)),
            sem((count, depth - 1)),
            sem((count, depth - 1)),
            sem((count, depth, blocks - 1)),
            sem((count, depth, blocks - 1)),
            sem((count, depth)),
            sem((count, depth)),
            sem((count + 1, max(depth, moves))),
        ],
        compiler_params=pltpu.CompilerParams(collective_id=cid, has_side_effects=True, vmem_limit_bytes=VMEM_LIMIT),
    )(*grads, *rows)


def normalize(values, gain, shift):
    center = jnp.mean(values, axis=-1, keepdims=True)
    offsets = values - center
    spread = jnp.mean(offsets * offsets, axis=-1, keepdims=True)
    return offsets * lax.rsqrt(spread + 1e-05) * gain + shift


def dot(left, right, at_left, at_right):
    return lax.dot_general(left, right, (((at_left,), (at_right,)), ((), ())), preferred_element_type=jnp.float32)


def swap(values, share, blocks, lanes, part):
    flat = blocks * lanes

    def number(blk, z, core):
        return blk * lanes + z * 2 + core

    pieces = [lax.dynamic_index_in_dim(values, part, 0, False)]
    for step in range(1, share):
        pairs = []
        for blk in range(blocks):
            for z in range(lanes // 2):
                for core in range(2):
                    other = (blk * 2 + core) ^ step
                    pairs.append((number(blk, z, core), number(other // 2, z, other % 2)))
        piece = lax.dynamic_index_in_dim(values, part ^ step, 0, False)
        pieces.append(lax.ppermute(piece, ("blk", "seq"), pairs))
    ordered = []
    for g in range(share):
        got = pieces[0]
        for step in range(1, share):
            got = jnp.where((part ^ step) == g, pieces[step], got)
        ordered.append(got)
    return ordered


def shards(sizes, tokens, seq_len, ln1_gain, ln1_shift, w_qkv, w_out, ln2_gain, ln2_shift, w_up, w_down, cotangent):
    blocks, lanes, seqs = sizes
    devices = blocks * lanes
    place = Place(*sizes)
    share, part = place.share, place.part
    model = tokens.shape[2]
    length = blocks * tokens.shape[1]
    rows = length // share
    owned = w_qkv.shape[0]
    cols = model // share
    wide = -(-cols // 128) * 128
    real = cols // 64

    grouped = w_qkv.reshape(owned, 3, share, cols)
    grouped = jnp.pad(grouped, ((0, 0), (0, 0), (0, 0), (0, wide - cols)))
    grouped = jnp.transpose(grouped, (2, 0, 1, 3)).reshape(share, owned, 3 * wide)
    vec = jnp.stack([ln1_gain, ln1_shift, ln2_gain, ln2_shift]).astype(jnp.float32)
    vec = jnp.pad(vec, ((0, 4), (0, 128 - owned)))
    vec = vec.at[4, :seqs].set(seq_len.astype(jnp.float32))
    outs = gather(sizes, tokens, cotangent, [grouped, vec, w_out, w_up, w_down])
    tok_all, cot_own, _, vec_all, out_full, up_full, down_full, qkv_cols = outs
    out_full, up_full, qkv_cols = [a.reshape(model, -1) for a in (out_full, up_full, qkv_cols)]
    down_full = down_full.reshape(-1, model)
    params = jnp.swapaxes(vec_all.reshape(devices, 8, 128)[:, :4, :owned], 0, 1).reshape(4, model)
    gain_one, shift_one, gain_two, shift_two = params
    lens = lax.dynamic_index_in_dim(vec_all[0], place.z, 0, False)[:, 4, :seqs].reshape(2 * seqs)
    my_len = lax.dynamic_index_in_dim(lens, place.seq, 0, False)

    inputs = tok_all.reshape(length, model).astype(jnp.float32)
    normed = normalize(inputs, gain_one, shift_one).astype(jnp.bfloat16)
    scale = jnp.where(jnp.arange(3 * wide) < wide, 0.125, 1.0)
    qkv = (dot(normed, qkv_cols, 1, 0) * scale).astype(jnp.bfloat16)
    att, lse = attend(qkv, 512, 512)
    att_parts = swap(att[:, :cols].reshape(share, rows, cols), share, blocks, lanes, part)
    att_own = jnp.concatenate(att_parts, -1)

    mine = lax.dynamic_slice_in_dim(tok_all.reshape(length, model), part * rows, rows, 0).astype(jnp.float32)
    positions = part * rows + jnp.arange(rows, dtype=jnp.int32)
    live = (positions.astype(jnp.float32) < my_len).astype(jnp.float32)[:, None]
    middle = mine + live * dot(att_own, out_full, 1, 0)
    normed_two = normalize(middle, gain_two, shift_two).astype(jnp.bfloat16)
    pre = dot(normed_two, up_full, 1, 0)
    hidden = jax.nn.gelu(pre, approximate=True).astype(jnp.bfloat16)
    result = (middle + dot(hidden, down_full, 1, 0)).astype(jnp.bfloat16)
    top = cot_own.reshape(rows, model)
    grad_down = dot(hidden, top, 0, 0).astype(jnp.bfloat16)
    grad_hidden = dot(top, down_full, 1, 1)
    pull = jax.vjp(lambda v: jax.nn.gelu(v, approximate=True), pre)[1]
    grad_pre = pull(grad_hidden)[0].astype(jnp.bfloat16)
    grad_up = dot(normed_two, grad_pre, 0, 0).astype(jnp.bfloat16)
    grad_two = dot(grad_pre, up_full, 1, 1)
    pull_two = jax.vjp(normalize, middle, gain_two, shift_two)[1]
    grad_norm, grad_gain_two, grad_shift_two = pull_two(grad_two)
    grad_mid = top.astype(jnp.float32) + grad_norm
    branch = (live * grad_mid).astype(jnp.bfloat16)
    grad_out = dot(att_own, branch, 0, 0).astype(jnp.bfloat16)
    g_att = dot(branch, out_full, 1, 1).astype(jnp.bfloat16)
    g_parts = swap(jnp.stack([g_att[:, g * cols : (g + 1) * cols] for g in range(share)]), share, blocks, lanes, part)
    g_heads = jnp.pad(jnp.concatenate(g_parts, 0), ((0, 0), (0, wide - cols)))
    g_qkv = attend_back(qkv, g_heads, att, lse, 512, 512)
    grad_qkv = dot(normed, g_qkv, 0, 0).astype(jnp.bfloat16)
    partial = dot(g_qkv * 1, qkv_cols, 1, 1)
    one_parts = swap(partial.astype(jnp.bfloat16).reshape(share, rows, model), share, blocks, lanes, part)
    grad_one = one_parts[0].astype(jnp.float32)
    for other in one_parts[1:]:
        grad_one = grad_one + other.astype(jnp.float32)
    pull_one = jax.vjp(normalize, mine, gain_one, shift_one)[1]
    grad_norm, grad_gain_one, grad_shift_one = pull_one(grad_one)
    grad_tokens = (grad_mid + grad_norm).astype(jnp.bfloat16)

    vec_grads = jnp.stack([grad_gain_one, grad_shift_one, grad_gain_two, grad_shift_two]).reshape(4, devices, owned)
    vec_grads = jnp.pad(jnp.swapaxes(vec_grads, 0, 1), ((0, 0), (0, 4), (0, 128 - owned)))

    def cut(values):
        return values.reshape((blocks, lanes // 2, 2, -1) + values.shape[1:])

    per_part = blocks // share
    done = reduce(
        sizes,
        [cut(grad_qkv), vec_grads.reshape(blocks, lanes // 2, 2, 8, 128), cut(grad_out), cut(grad_up), cut(grad_down)],
        ["columns", "rows", "rows", "rows", "rows"],
        [result.reshape(per_part, -1, model), grad_tokens.reshape(per_part, -1, model)],
        1,
    )
    sum_qkv, sum_vec, sum_out, sum_up, sum_down, result, grad_tokens = done
    sum_qkv = jnp.transpose(sum_qkv.reshape(share, owned, 3, wide)[..., :cols], (1, 2, 0, 3)).reshape(owned, 3 * model)
    return (
        result,
        grad_tokens.astype(jnp.float32),
        sum_vec[0, :owned],
        sum_vec[1, :owned],
        sum_qkv,
        sum_out,
        sum_vec[2, :owned],
        sum_vec[3, :owned],
        sum_up,
        sum_down,
    )


def solution(mesh):
    blocks, lanes = mesh.shape["blk"], mesh.shape["seq"]
    whole = P(("blk", "seq"))
    rows = P(("blk", "seq"), None)
    tokens = P("seq", "blk", None)

    def run(*args):
        seqs = args[0].shape[0] // lanes
        return jax.shard_map(
            functools.partial(shards, (blocks, lanes, seqs)),
            mesh=mesh,
            in_specs=(tokens, P("seq"), whole, whole, rows, rows, whole, whole, rows, rows, tokens),
            out_specs=(tokens, tokens, whole, whole, rows, rows, whole, whole, rows, rows),
            check_vma=False,
        )(*args)

    return run
```

time: 1340 us -> 527 us (0.39)
  waiting for transfers between devices: 653 us -> 0.39 us
  Pallas kernels: 0 us -> 363 us
  matrix products: 451 us -> 93.8 us
  blocking collectives: 81.8 us -> 0 us
  local copies, waits for them, and re-layouts: 62.2 us -> 20.4 us
  other arithmetic: 75.9 us -> 36.5 us
    reduce_scatter x5 -> x0, waiting for transfers between devices: 498 us -> none  [the longest x1 142 us: shards(): lax.psum_scatter(grad_up, ('blk', 'seq'), scatter_dimension=0, tiled=True)]
    pallas_call x0 -> x4, Pallas kernels: none -> 363 us  [the longest x1 119 us: reduce(): pl.pallas_call(functools.partial(reduce_kernel, sizes, kinds, moves), out...]
    dot_general x19 -> x12, matrix products: 451 us -> 93.8 us  [dot(): lax.dot_general(left, right, (((at_left,), (at_right,)), ((), ())), prefe...]
    all_gather x6 -> x0, waiting for transfers between devices: 152 us -> none  [the longest x1 62.2 us: shards(): lax.all_gather(key_rows, 'blk', axis=1, tiled=True)]
    unnamed x2 -> x0, blocking collectives: 81.8 us -> none
    reduce_sum x1 -> x0, other arithmetic: 47.1 us -> none  [attend_piece(): denom = jnp.sum(weights, axis=-1)]
    all_gather x2 -> x0, local copies, waits for them, and re-layouts: 17.4 us -> none  [the longest x1 8.71 us: shards(): lax.all_gather(key_rows, 'blk', axis=1, tiled=True)]
    reshape x3 -> x5, local copies, waits for them, and re-layouts: 19.7 us -> 3.61 us  [the longest x1 1.02 us: shards(): sum_qkv.reshape(share, owned, 3, wide)[..., :cols]]
  transfers between devices with their start and end apart: 11 -> 3, of which waited for: 9 -> 1; matrix products, arithmetic and copies ran while one was open for 22% -> 7% of each run, Pallas kernels for 0% -> 0%
where the time goes in v1:
time: 527 us; the launch traced here: 517 us
  Pallas kernels  363 us (69%)
  matrix products  93.8 us (18%)
  other arithmetic  36.5 us (7%)
  local copies, waits for them, and re-layouts  20.4 us (4%)
    pallas_call x1, Pallas kernels, reduce(): pl.pallas_call(functools.partial(reduce_kernel, sizes, kinds, moves), out...  119 us
    pallas_call x1, Pallas kernels, gather(): pl.pallas_call(functools.partial(gather_kernel, sizes, [s.shape for s in...  108 us
    dot_general x12, matrix products, dot(): lax.dot_general(left, right, (((at_left,), (at_right,)), ((), ())), prefe...  93.8 us
    pallas_call x1, Pallas kernels, attend_back(): pl.pallas_call(functools.partial(bwd_kernel, bq, bk, pairs), grid=(pairs,...  79.9 us
    pallas_call x1, Pallas kernels, attend(): pl.pallas_call(functools.partial(fwd_kernel, bq, bk), grid=(pairs,), out_...  55.7 us
    reduce_sum x2, other arithmetic, normalize(): offsets = values - center  14.9 us
  transfers between devices with their start and end apart: 3, of which 1 were waited for; matrix products, arithmetic and copies ran while one was open for 7% of the time, Pallas kernels for 0%

profile of v1, /device:TPU:0, one launch (start us, length us, event | category | flops | bytes accessed | tf_op | source)
XLA Modules:
  0.0 517.3 jit_solution(7936901937482111756)
XLA Ops:
  4.6 108.5 %shard_map.186 = (bf16[4,512,768]{2,1,0:T(8,128)(2,1)}, bf16[2,512,768]{2,1,0:T(8,128)(2,1)}, bf16[4,4,2,2,24,1152]{5,4,3,2,1,0:T(8,128)(2,1)}, f32[4,4,2,8,128]...) custom-call(bf16[2,512,768]{2,1,0:T(8,128)(2,1)} %refs_0_.1, ...), custom_call_target="tpu_custom_call" | custom-call | tf_op jit(solution)/shard_map/pallas_call | solution.py:426
  113.1 2.5 convert_reduce_fusion
  118.7 5.8 %fusion.7.q_ref.k_ref.v_ref = bf16[2048,1152]{1,0:T(8,128)(2,1)} fusion(bf16[2048,768]{1,0:T(8,128)(2,1)S(1)} %bitcast.105, bf16[768,1152]{1,0:T(8,128)(2,1)S(1)} %bitcast.131, f32[1152]{0:T(1024)S(1)} %fusion.31), kind=kOutput, calls=%fused_computation.13 | convolution fusion | flops 3628597248 | bytes 9638400 | tf_op jit(solution)/shard_map/dot_general | solution.py:653
  124.5 55.7 %shard_map.187 = (bf16[2048,384]{1,0:T(8,128)(2,1)}, f32[3,8,2048]{2,1,0:T(8,128)}) custom-call(bf16[2048,1152]{1,0:T(8,128)(2,1)} %fusion.7.q_ref.k_ref.v_ref, bf16[2048,1152]{1,0:T(8,128)(2,1)} %fusion.7.q_ref.k_ref.v_ref, bf16[2048,1152]{1,0:T(8,128)(2,1)} %fusion.7.q_ref.k_ref.v_ref), custom_call_target="tpu_custom_call" | custom-call | tf_op jit(solution)/shard_map/pallas_call | solution.py:87
  180.2 2.1 dynamic-slice_bitcast_fusion.1
  185.1 1.5 bitcast_select_fusion.3
  186.7 1.5 fusion.56
  190.5 8.6 %fusion.53 = f32[1024,3072]{1,0:T(8,128)} fusion(bf16[768,3072]{1,0:T(8,128)(2,1)S(1)} %bitcast.124, f32[1024,768]{1,0:T(8,128)S(1)} %get-tuple-element.87, f32[768]{0:T(1024)S(1)} %add.153, f32[768]{0:T(1024)S(1)} %mul.234, f32[1024]{0:T(1024)S(1)} %fusion.38, f32[1024]{0:T(1024)S(1)} %broadcast_multiply_fusion.2), kind=kOutput, calls=%fused_computation.120 | convolution fusion | flops 4835770368 | bytes 20461568 | tf_op jit(solution)/shard_map/dot_general | solution.py:653
  199.1 11.4 %add_convert_fusion.3 = bf16[1024,768]{1,0:T(8,128)(2,1)} fusion(f32[1024,768]{1,0:T(8,128)S(1)} %get-tuple-element.87, bf16[3072,768]{1,0:T(8,128)(2,1)S(1)} %bitcast.128, f32[1024,3072]{1,0:T(8,128)} %fusion.53), kind=kOutput, calls=%fused_computation.39 | convolution fusion | flops 4861722624 | bytes 22020096 | tf_op jit(solution)/shard_map/dot_general | solution.py:653
  210.5 15.3 %fusion.6 = bf16[1024,3072]{1,0:T(8,128)(2,1)} fusion(f32[1024,3072]{1,0:T(8,128)} %fusion.53, bf16[1024,768]{1,0:T(8,128)(2,1)S(1)} %bitcast.98, bf16[3072,768]{1,0:T(8,128)(2,1)S(1)} %bitcast.129), kind=kOutput, calls=%fused_computation.8 | convolution fusion | flops 4894752768 | bytes 25165824 | tf_op jit(solution)/shard_map/dot_general | solution.py:653
  225.8 7.8 %multiply_reduce_fusion = (f32[768]{0:T(1024)S(1)}, f32[1024]{0:T(1024)S(1)}, f32[768]{0:T(1024)S(1)}, f32[1024,768]{1,0:T(8,128)S(1)}) fusion(f32[1024,768]{1,0:T(8,128)S(1)} %get-tuple-element.87, f32[1024]{0:T(1024)S(1)} %fusion.38, f32[1024]{0:T(1024)S(1)} %broadcast_multiply_fusion.2, f32[768]{0:T(1024)S(1)} %mul.234, bf16[1024,3072]{1,0:T(8,128)(2,1)} %fusion.6, ...), kind=kOutput, calls=%fused_computation.40 | convolution fusion | flops 4838126592 | bytes 17323008 | tf_op jit(solution)/shard_map/dot_general | solution.py:653
  233.6 12.9 %fusion.54 = (f32[1024]{0:T(1024)S(1)}, f32[1024,768]{1,0:T(8,128)S(1)}) fusion(f32[1024]{0:T(1024)S(1)} %multiply_multiply_fusion.3, f32[1024,768]{1,0:T(8,128)S(1)} %get-tuple-element.87, f32[1024]{0:T(1024)S(1)} %broadcast_multiply_fusion.2, f32[1024]{0:T(1024)S(1)} %fusion.38, f32[1024,768]{1,0:T(8,128)S(1)} %get-tuple-element.88, f32[768]{0:T(1024)S(1)} %mul.234), kind=kLoop, calls=%fused_computation.121 | loop fusion | flops 5504000 | bytes 9456640 | tf_op jit(solution)/shard_map/transpose(jvp())/reduce_sum | solution.py:647
  250.6 11.7 %convolution_convert_fusion = bf16[3072,768]{1,0:T(8,128)(2,1)} fusion(bf16[1024,768]{1,0:T(8,128)(2,1)S(1)} %bitcast.99, f32[1024,3072]{1,0:T(8,128)} %fusion.53), kind=kOutput, calls=%fused_computation.21 | convolution fusion | flops 4862509056 | bytes 18874368 | tf_op jit(solution)/shard_map/dot_general | solution.py:653
  264.1 79.9 %shard_map.188 = bf16[2048,1152]{1,0:T(8,128)(2,1)} custom-call(bf16[2048,1152]{1,0:T(8,128)(2,1)} %fusion.7.q_ref.k_ref.v_ref, bf16[2048,1152]{1,0:T(8,128)(2,1)} %fusion.7.q_ref.k_ref.v_ref, bf16[2048,1152]{1,0:T(8,128)(2,1)} %fusion.7.q_ref.k_ref.v_ref, bf16[2048,384]{1,0:T(8,128)(2,1)} %pad_maximum_fusion.1.g_ref, ...), custom_call_target="tpu_custom_call" | custom-call | tf_op jit(solution)/shard_map/pallas_call | solution.py:170
  344.0 7.2 %convolution_convert_fusion.2 = bf16[2048,768]{1,0:T(8,128)(2,1)S(1)} fusion(bf16[2048,1152]{1,0:T(8,128)(2,1)} %shard_map.188, bf16[768,1152]{1,0:T(8,128)(2,1)} %bitcast.130), kind=kOutput, calls=%fused_computation.32 | convolution fusion | flops 3625451520 | bytes 9633792 | tf_op jit(solution)/shard_map/dot_general | solution.py:653
  352.7 2.2 copy-done.4
  354.8 10.1 %convolution_convert_fusion.1 = bf16[768,3072]{1,0:T(8,128)(2,1)} fusion(bf16[1024,3072]{1,0:T(8,128)(2,1)} %fusion.6, f32[1024,768]{1,0:T(8,128)S(1)} %copy-done.4, f32[768]{0:T(1024)S(1)} %add.153, f32[768]{0:T(1024)S(1)} %mul.234, f32[1024]{0:T(1024)S(1)} %fusion.38, f32[1024]{0:T(1024)S(1)} %broadcast_multiply_fusion.2), kind=kOutput, calls=%fused_computation.22 | convolution fusion | flops 4838129664 | bytes 14170112 | tf_op jit(solution)/shard_map/dot_general | solution.py:653
  365.1 4.4 convolution_convert_fusion.5
  369.5 8.5 %convolution_convert_fusion.3 = bf16[768,1152]{1,0:T(8,128)(2,1)} fusion(bf16[2048,1152]{1,0:T(8,128)(2,1)} %shard_map.188, bf16[2048,768]{1,0:T(8,128)(2,1)S(1)} %bitcast.94, f32[768]{0:T(1024)S(1)} %add.136, f32[768]{0:T(1024)S(1)} %mul.218, f32[2048]{0:T(1024)S(1)} %bitcast.117, f32[2048]{0:T(1024)S(1)} %bitcast.116), kind=kOutput, calls=%fused_computation.33 | convolution fusion | flops 3634200576 | bytes 9656320 | tf_op jit(solution)/shard_map/dot_general | solution.py:653
  378.0 3.1 fusion.21
  381.2 2.1 fusion.52
  383.5 3.1 add_convert_fusion.2
  387.5 119.3 %shard_map.189 = (f32[2,24,1152]{2,1,0:T(8,128)}, f32[8,128]{1,0:T(8,128)}, f32[24,768]{1,0:T(8,128)}, f32[24,3072]{1,0:T(8,128)}, f32[96,768]{1,0:T(8,128)}, /*...) custom-call(bf16[4,4,2,24,1152]{4,3,2,1,0:T(8,128)(2,1)} %bitcast.108, f32[4,4,2,8,128]{4,3,2,1,0:T(8,128)} %bitcast.113, ...), custom_call_target="tpu_custom_call" | custom-call | tf_op jit(solution)/shard_map/pallas_call | solution.py:618
  510.3 3.4 convert_element_type.117
  (112 shorter events, 27.0 us)
Async XLA Ops:
  113.1 2.8 copy-start
  113.1 3.9 copy-start.16
  182.3 2.8 collective-permute-start
  183.2 3.5 copy-start.19
  186.7 1.6 copy-start.11
  186.7 1.6 copy-start.12
  186.7 3.3 slice-start
  186.7 3.8 slice-start.1
  188.3 45.4 %copy-start.3 = (f32[1024,768]{1,0:T(8,128)}, f32[1024,768]{1,0:T(8,128)S(1)}, u32[]{:S(2)}) copy-start(f32[1024,768]{1,0:T(8,128)S(1)} %get-tuple-element.87) | copy-start | bytes 9437188
  188.3 10.8 %slice-start.2 = ((s8[4718592]{0:T(1024)(128)(4,1)}), s8[4194304]{0:T(1024)(128)(4,1)S(1)}, s32[]{:S(2)}) async-start(s8[4718592]{0:T(1024)(128)(4,1)} %bitcast.126), calls=%async_computation.2 | async-start | bytes 8388608
  190.5 8.6 %slice-start.3 = ((s8[4718592]{0:T(1024)(128)(4,1)}), s8[524288]{0:T(1024)(128)(4,1)S(1)}, s32[]{:S(2)}) async-start(s8[4718592]{0:T(1024)(128)(4,1)} %bitcast.126), calls=%async_computation.3 | async-start | bytes 1048576
  199.1 11.4 %copy-start.5 = (bf16[2,512,768]{2,1,0:T(8,128)(2,1)S(1)}, bf16[2,512,768]{2,1,0:T(8,128)(2,1)}, u32[]{:S(2)}) copy-start(bf16[2,512,768]{2,1,0:T(8,128)(2,1)} %get-tuple-element.41) | copy-start | bytes 4718596
  246.5 1.7 copy-start.1
  250.2 12.2 %collective-permute-start.1 = (bf16[1024,384]{1,0:T(8,128)(2,1)S(1)}, bf16[1024,384]{1,0:T(8,128)(2,1)S(1)}, u32[]{:S(2)}, u32[]{:S(2)}) collective-permute-start(bf16[1024,384]{1,0:T(8,128)(2,1)S(1)} %fusion.30), channel_id=1, source_target_pairs={{0,1},{1,0},{2,3},{3,2},{4,5},{5,4},{6,7},{7,6},{8,9},{9,8},{10,11... | collective-permute-start | bytes 2359304 | tf_op jit(solution)/shard_map/ppermute | solution.py:671
  351.2 13.7 %copy-start.7 = (bf16[2048,768]{1,0:T(8,128)(2,1)}, bf16[2048,768]{1,0:T(8,128)(2,1)S(1)}, u32[]{:S(2)}) copy-start(bf16[2048,768]{1,0:T(8,128)(2,1)S(1)} %convolution_convert_fusion.2) | copy-start | bytes 9437188
  351.2 3.6 copy-start.4
  352.5 25.5 %collective-permute-start.2 = (bf16[1024,768]{1,0:T(8,128)(2,1)}, bf16[1024,768]{1,0:T(8,128)(2,1)}, u32[]{:S(2)}, u32[]{:S(2)}) collective-permute-start(bf16[1024,768]{1,0:T(8,128)(2,1)} %dynamic-slice_bitcast_fusion), channel_id=1, source_target_pairs={{0,1},{1,0},{2,3},{3,2},{4,5},{5,4},{6,7},{7,6},{8,9},{9,8},{10,11... | collective-permute-start | bytes 4718600 | tf_op jit(solution)/shard_map/ppermute | solution.py:671
  369.5 8.5 %copy-start.8 = (bf16[2048,768]{1,0:T(8,128)(2,1)S(1)}, bf16[2048,768]{1,0:T(8,128)(2,1)}, u32[]{:S(2)}) copy-start(bf16[2048,768]{1,0:T(8,128)(2,1)} %copy-done.7) | copy-start | bytes 9437188
  381.2 2.1 copy-start.2
  381.2 2.3 copy-start.6
  506.8 6.8 %copy-start.9 = (bf16[2,512,768]{2,1,0:T(8,128)(2,1)S(1)}, bf16[2,512,768]{2,1,0:T(8,128)(2,1)}, u32[]{:S(2)}) copy-start(bf16[2,512,768]{2,1,0:T(8,128)(2,1)} %get-tuple-element.99) | copy-start | bytes 4718596
  510.2 4.5 copy-start.15
  510.2 5.2 copy-start.14
  510.3 5.9 %copy-start.13 = (f32[96,768]{1,0:T(8,128)S(1)}, f32[96,768]{1,0:T(8,128)}, u32[]{:S(2)}) copy-start(f32[96,768]{1,0:T(8,128)} %get-tuple-element.108) | copy-start | bytes 884740
  (3 other events, 3.5 us)
